TPU v7x, 128 devices: a whole 4x4x4 slice. The times are simulated.
128 devices in a mesh: group: 16 (over x, z), local: 8 (over y, core).
Axes of the slice: x: 4, y: 4, z: 4, core: 2. Of those that a mesh axis runs over, the one named last changes fastest.
Arguments:
- tokens: bfloat16 [16384, 4096], P(('group', 'local')), may hold values from -6 to 6
- expert_ids: int32 [16384, 2], P(('group', 'local')), may hold values from 0 to 63, all different within a row; in each aligned block of 128 rows (0 to 127, 128 to 255, ...) at most 6 rows name the same one
- gate_scores: float32 [16384, 2], P(('group', 'local')), may hold values from 0.1 to 1
- w_gate: bfloat16 [128, 4096, 768], P(('group', 'local')), may hold values from -0.09375 to 0.09375
- w_up: bfloat16 [128, 4096, 768], P(('group', 'local')), may hold values from -0.09375 to 0.09375
- w_down: bfloat16 [128, 768, 4096], P(('group', 'local')), may hold values from -0.15625 to 0.15625
Outputs:
- mixed: bfloat16 [16384, 4096], P(('group', 'local'))
Inputs may be any that keep to these rules, and one draw needn't show every extreme that they name: `expert_ids`: among the 128 rows of one device (aligned blocks), each row names 2 different experts, and no expert is named by more than 6 rows of the block; some expert reaches 6 rows.
All inputs are finite; a program needn't handle non-finite values.
Results may differ from a plain program's by a relative error of at most 0.0065.
Values may be sent and summed in bfloat16 or wider, within the bound.
A program may use at most 128 MiB of HBM per device.

v0:
```python
import jax
import jax.numpy as jnp
from jax import lax
from jax.sharding import PartitionSpec as P


def body(tokens, expert_ids, gate_scores, w_gate, w_up, w_down):
    rows, width = tokens.shape
    top = expert_ids.shape[1]
    n_group = lax.axis_size("group")
    n_local = lax.axis_size("local")
    devices = n_group * n_local
    experts = devices // 2
    capacity = max(2, 2 * ((3 * rows * top + 4 * experts - 1) // (4 * experts)))
    assigned = rows * top
    weights = gate_scores / jnp.sum(gate_scores, axis=1, keepdims=True)
    flat_ids = expert_ids.reshape(-1)
    onehot = (flat_ids[:, None] == jnp.arange(experts, dtype=jnp.int32)[None, :]).astype(jnp.int32)
    before = jnp.cumsum(onehot, axis=0) - onehot
    slot_rank = jnp.sum(before * onehot, axis=1)
    place = flat_ids * capacity + slot_rank
    source = jnp.full((experts * capacity,), assigned, jnp.int32)
    source = source.at[place].set(jnp.arange(assigned, dtype=jnp.int32))
    padded_tokens = jnp.concatenate([tokens, jnp.zeros((1, width), tokens.dtype)], axis=0)
    outgoing = padded_tokens[source // top].reshape(experts, capacity, width)
    doubled = jnp.repeat(outgoing, 2, axis=0)
    arrived = lax.all_to_all(doubled, ("group", "local"), split_axis=0, concat_axis=0, tiled=True)
    leading = arrived.shape[:-1]
    flat_rows = arrived.reshape(-1, width)
    gate = jnp.dot(flat_rows, w_gate[0], preferred_element_type=jnp.float32)
    upper = jnp.dot(flat_rows, w_up[0], preferred_element_type=jnp.float32)
    hidden = (jax.nn.silu(gate) * upper).astype(jnp.bfloat16)
    part = jnp.dot(hidden, w_down[0], preferred_element_type=jnp.float32).astype(jnp.bfloat16)
    partial_value = part.reshape(leading + (width,))
    returned = lax.all_to_all(
        partial_value, ("group", "local"), split_axis=0, concat_axis=0, tiled=True
    )
    returned = lax.optimization_barrier(returned.reshape(experts, 2, capacity, width))
    summed = returned[:, 0].astype(jnp.float32) + returned[:, 1].astype(jnp.float32)
    expert_out = summed.astype(jnp.bfloat16).reshape(experts * capacity, width)
    expert_out = lax.optimization_barrier(expert_out)
    picked = expert_out[place].astype(jnp.float32).reshape(rows, top, width)
    mixed = jnp.sum(picked * weights[:, :, None], axis=1)
    return mixed.astype(jnp.bfloat16)


def solution(mesh):
    in_specs = (
        P(("group", "local"), None),
        P(("group", "local"), None),
        P(("group", "local"), None),
        P(("group", "local"), None, None),
        P(("group", "local"), None, None),
        P(("group", "local"), None, None),
    )
    out_specs = P(("group", "local"), None)
    return jax.shard_map(body, mesh=mesh, in_specs=in_specs, out_specs=out_specs, check_vma=False)
```

profile of v0, /device:TPU:1, one launch (start us, length us, event | category | flops | bytes accessed | tf_op | source)
XLA Modules:
  0.0 322.9 jit_solution(2539052579262617976)
XLA Ops:
  0.0 0.8 copy.11
  0.9 0.1 eq.25
  1.1 0.7 broadcast_multiply_fusion
  1.8 0.6 reduce-window.6
  2.4 0.2 slice_reduce_fusion
  2.7 0.1 mul.36
  3.0 1.4 scatter_custom_fusion
  4.4 1.3 concatenate.3
  5.8 4.0 %gather_fusion = bf16[384,4096]{1,0:T(8,128)(2,1)} fusion(bf16[129,4096]{1,0:T(8,128)(2,1)S(1)} %concatenate.3, s32[1024]{0:T(1024)S(1)} %pad_clamp_fusion.1), kind=kCustom, calls=%fused_computation | custom fusion | bytes 6292992 | tf_op jit(solution)/shard_map/gather | solution.py:25
  9.8 5.7 %reshape.75 = bf16[64,6,4096]{2,1,0:T(8,128)(2,1)} reshape(bf16[384,4096]{1,0:T(8,128)(2,1)} %gather_fusion) | data formatting | bytes 6291456 | tf_op jit(solution)/shard_map/reshape | solution.py:25
  15.5 6.5 %broadcast_in_dim.8 = bf16[64,2,6,4096]{3,2,1,0:T(8,128)(2,1)} broadcast(bf16[64,6,4096]{2,1,0:T(8,128)(2,1)} %reshape.75), dimensions={0,2,3} | broadcast | bytes 9437184 | tf_op jit(solution)/shard_map/broadcast_in_dim | solution.py:26
  21.9 110.0 %all_to_all.10 = bf16[128,6,4096]{2,1,0:T(8,128)(2,1)} all-to-all(bf16[128,6,4096]{2,1,0:T(8,128)(2,1)} %bitcast.47), channel_id=1, replica_groups=mesh['group'=16,'local'=8] {'group','local'}, dimensions={0} | all-to-all | bytes 12582912 | tf_op jit(solution)/shard_map/all_to_all | solution.py:27
  132.0 10.3 %reshape.77 = bf16[768,4096]{1,0:T(8,128)(2,1)} reshape(bf16[128,6,4096]{2,1,0:T(8,128)(2,1)} %all_to_all.10) | data formatting | bytes 12582912 | tf_op jit(solution)/shard_map/reshape | solution.py:29
  142.2 9.1 %fusion.3 = f32[768,768]{1,0:T(8,128)S(1)} fusion(bf16[768,4096]{1,0:T(8,128)(2,1)} %reshape.77, bf16[1,4096,768]{2,1,0:T(8,128)(2,1)} %param.9), kind=kOutput, calls=%fused_computation.8 | convolution fusion | flops 4831838208 | bytes 14942208 | tf_op jit(solution)/shard_map/dot_general | solution.py:30
  151.4 8.0 %multiply_convert_fusion = bf16[768,768]{1,0:T(8,128)(2,1)S(1)} fusion(f32[768,768]{1,0:T(8,128)S(1)} %fusion.3, bf16[768,4096]{1,0:T(8,128)(2,1)S(1)} %copy-done, bf16[1,4096,768]{2,1,0:T(8,128)(2,1)} %param.10), kind=kOutput, calls=%fused_computation.13 | convolution fusion | flops 4835377152 | bytes 16121856 | tf_op jit(solution)/shard_map/dot_general | solution.py:31
  159.4 9.8 %convolution_convert_fusion = bf16[768,4096]{1,0:T(8,128)(2,1)} fusion(bf16[768,768]{1,0:T(8,128)(2,1)S(1)} %multiply_convert_fusion, bf16[1,768,4096]{2,1,0:T(8,128)(2,1)} %param.11), kind=kOutput, calls=%fused_computation.4 | convolution fusion | flops 4834983936 | bytes 13762560 | tf_op jit(solution)/shard_map/dot_general | solution.py:33
  169.2 10.1 %reshape.78 = bf16[128,6,4096]{2,1,0:T(8,128)(2,1)} reshape(bf16[768,4096]{1,0:T(8,128)(2,1)} %convolution_convert_fusion) | data formatting | bytes 12582912 | tf_op jit(solution)/shard_map/reshape | solution.py:34
  179.3 9.2 %all-to-all-start.1 = ((bf16[128,6,4096]{2,1,0:T(8,128)(2,1)}), bf16[128,6,4096]{2,1,0:T(8,128)(2,1)}, u32[]{:S(2)}, u32[]{:S(2)}) async-start(bf16[128,6,4096]{2,1,0:T(8,128)(2,1)} %reshape.78), calls=%async_computation.1 | async-start | bytes 16777216 | tf_op jit(solution)/shard_map/all_to_all | solution.py:35
  188.7 106.1 %all-to-all-done.1 = bf16[128,6,4096]{2,1,0:T(8,128)(2,1)} async-done(((bf16[128,6,4096]{2,1,0:T(8,128)(2,1)}), bf16[128,6,4096]{2,1,0:T(8,128)(2,1)}, u32[]{:S(2)}, u32[]{:S(2)}) %all-to-all-start.1) | async-done | bytes 6291488 | tf_op jit(solution)/shard_map/all_to_all | solution.py:35
  294.8 5.7 %add_convert_fusion = bf16[64,1,6,4096]{3,2,0,1:T(8,128)(2,1)} fusion(bf16[64,2,6,4096]{3,2,1,0:T(8,128)(2,1)} %bitcast.7), kind=kLoop, calls=%fused_computation.3 | loop fusion | flops 6291456 | bytes 9437184 | tf_op jit(solution)/shard_map/convert_element_type | solution.py:40
  300.5 4.2 %convert_element_type.47 = bf16[384,4096]{1,0:T(8,128)(2,1)S(1)} reshape(bf16[64,1,6,4096]{3,2,0,1:T(8,128)(2,1)} %add_convert_fusion) | data formatting | bytes 6291456 | tf_op jit(solution)/shard_map/convert_element_type | solution.py:40
  304.6 3.2 gather_fusion.1
  307.8 5.4 %reshape.80 = f32[128,2,4096]{2,1,0:T(2,128)} reshape(bf16[256,4096]{1,0:T(8,128)(2,1)} %gather_fusion.1) | data formatting | bytes 6291456 | tf_op jit(solution)/shard_map/convert_element_type | solution.py:42
  313.2 9.6 %multiply_reduce_fusion = bf16[128,4096]{1,0:T(8,128)(2,1)} fusion(f32[128,2,4096]{2,1,0:T(2,128)} %reshape.80, f32[128,2]{1,0:T(8,128)S(1)} %copy.16), kind=kLoop, calls=%fused_computation.12 | loop fusion | flops 1572864 | bytes 5243904 | tf_op jit(solution)/shard_map/reduce_sum | solution.py:43
  (18 shorter events, 0.6 us)
Async XLA Ops:
  142.2 9.1 %copy-start = (bf16[768,4096]{1,0:T(8,128)(2,1)S(1)}, bf16[768,4096]{1,0:T(8,128)(2,1)}, u32[]{:S(2)}) copy-start(bf16[768,4096]{1,0:T(8,128)(2,1)} %reshape.77) | copy-start | bytes 18874372
  179.3 9.2 %copy-start.1 = (f32[128,2]{0,1:T(2,128)S(1)}, f32[128,2]{0,1:T(2,128)}, u32[]{:S(2)}) copy-start(f32[128,2]{0,1:T(2,128)} %param.8) | copy-start | bytes 3076
  179.3 115.5 %all-to-all-start.1 = ((bf16[128,6,4096]{2,1,0:T(8,128)(2,1)}), bf16[128,6,4096]{2,1,0:T(8,128)(2,1)}, u32[]{:S(2)}, u32[]{:S(2)}) async-start(bf16[128,6,4096]{2,1,0:T(8,128)(2,1)} %reshape.78), calls=%async_computation.1 | async-start | bytes 16777216 | tf_op jit(solution)/shard_map/all_to_all | solution.py:35
where the time goes:
time: 324 us; the launch traced here: 323 us
  blocking collectives  110 us (34%)
  waiting for transfers between devices  106 us (33%)
  local copies, waits for them, and re-layouts  53.7 us (17%)
  matrix products  26.9 us (8%)
  other arithmetic  16.8 us (5%)
  starting transfers between devices  9.2 us (3%)
    all_to_all x1, blocking collectives, body(): lax.all_to_all(doubled, ('group', 'local'), split_axis=0, concat_axis=0,...  110 us
    all_to_all x1, waiting for transfers between devices, body(): lax.all_to_all(partial_value, ('group', 'local'), split_axis=0, concat_ax...  106 us
    reshape x1, local copies, waits for them, and re-layouts, body(): flat_rows = arrived.reshape(-1, width)  10.3 us
    reshape x1, local copies, waits for them, and re-layouts, body(): partial_value = part.reshape(leading + (width,))  10.1 us
    dot_general x1, matrix products, body(): jnp.dot(hidden, w_down[0], preferred_element_type=jnp.float32)  9.82 us
    reduce_sum x1, other arithmetic, body(): mixed = jnp.sum(picked * weights[:, :, None], axis=1)  9.64 us
    all_to_all x1, starting transfers between devices, body(): lax.all_to_all(partial_value, ('group', 'local'), split_axis=0, concat_ax...  9.2 us
    dot_general x1, matrix products, body(): gate = jnp.dot(flat_rows, w_gate[0], preferred_element_type=jnp.float32)  9.09 us
  transfers between devices with their start and end apart: 1, of which 1 were waited for; matrix products, arithmetic and copies ran while one was open for 0% of the time, Pallas kernels for 0%

commit v1 on v0

v1 whole, which is shorter than its diff:
```python
import jax
import jax.numpy as jnp
from jax import lax
from jax.experimental import pallas as pl
from jax.experimental.pallas import tpu as pltpu
from jax.sharding import PartitionSpec as P

MESH = pl.DeviceIdType.MESH
BF16, F32 = jnp.bfloat16, jnp.float32

SIDE = 4
CHIPS = SIDE**3
CAP = 6
GROUPS = 4
SLOTS = CHIPS // GROUPS
CHUNK = 512
PIECES = 8
PAIRS = CAP // 2
LANES = PAIRS * CHUNK
OWN = SLOTS * CAP
STRIDE = 22


def shift_of(slot):
    return 1 + lax.rem(slot * STRIDE, CHIPS - 1)


def kernel(
    ids, scores, tok_hbm, gate_hbm, up_hbm, down_hbm, out,
    tok, w_gate, w_up, w_down,
    sent, got, rows, hidden, part_own, part_out, part_in, answer, back,
    pick, mixing, spread, unspread, stage, flat, total,
    load_sem, there_send, there_recv, row_send, row_recv, part_send, part_recv, back_send, back_recv, own_sem,
):
    group, local = lax.axis_index("group"), lax.axis_index("local")
    x, z = lax.div(group, SIDE), lax.rem(group, SIDE)
    y, core = lax.div(local, 2), lax.rem(local, 2)
    twin = (group, local + 1 - 2 * core)

    def partner(slot, sign):
        shift = shift_of(slot)
        far_x = lax.rem(x + SIDE + sign * lax.div(shift, SIDE * SIDE), SIDE)
        far_y = lax.rem(y + SIDE + sign * lax.rem(lax.div(shift, SIDE), SIDE), SIDE)
        far_z = lax.rem(z + SIDE + sign * lax.rem(shift, SIDE), SIDE)
        return (far_x * SIDE + far_z, far_y * 2 + core)

    def loads():
        pairs = ((tok_hbm, tok), (gate_hbm.at[0], w_gate), (up_hbm.at[0], w_up), (down_hbm.at[0], w_down))
        return [pltpu.make_async_copy(a, b, load_sem.at[n]) for n, (a, b) in enumerate(pairs)]

    barrier = pltpu.get_barrier_semaphore()

    def greet(slot, carry):
        pl.semaphore_signal(barrier, inc=1, device_id=partner(slot, 1), device_id_type=MESH)
        return carry

    lax.fori_loop(0, CHIPS - 1, greet, 0)
    pl.semaphore_signal(barrier, inc=1, device_id=twin, device_id_type=MESH)
    for copy in loads():
        copy.start()

    n = 2 * CHIPS
    row = lax.broadcasted_iota(jnp.int32, (n, n), 0)
    column = lax.broadcasted_iota(jnp.int32, (n, n), 1)
    slot, odd = lax.shift_right_logical(row, 1), row & 1
    shift = jnp.where(slot == CHIPS - 1, 0, shift_of(slot))
    expert = ((x + lax.shift_right_logical(shift, 4)) & 3) * 16 + ((z + shift) & 3) * 4 + ((y + lax.shift_right_logical(shift, 2)) & 3)
    first, second = expert == ids[0:1, :], expert == ids[1:2, :]
    chosen = jnp.where(first | second, 1.0, 0.0)
    earlier = jnp.where(row < column, 1.0, 0.0).astype(BF16)
    rank = jnp.dot(chosen.astype(BF16), earlier, preferred_element_type=F32)
    scale = scores[0:1, :] + scores[1:2, :]
    weight = jnp.where(first, scores[0:1, :] / scale, 0.0) + jnp.where(second, scores[1:2, :] / scale, 0.0)
    for j in range(PAIRS):
        here = jnp.where(rank == (2 * j + odd).astype(F32), chosen, 0.0)
        high = (here * weight).astype(BF16)
        low = (here * weight - high.astype(F32)).astype(BF16)
        for q in range(GROUPS):
            part = slice(2 * SLOTS * q, 2 * SLOTS * (q + 1))
            place = slice(2 * SLOTS * j, 2 * SLOTS * (j + 1))
            pick[q, place, :] = here[part].astype(BF16)
            mixing[0, q, place, :] = high[part]
            mixing[1, q, place, :] = low[part]

    m = 2 * SLOTS * PIECES
    a = lax.broadcasted_iota(jnp.int32, (m, m), 0)
    b = lax.broadcasted_iota(jnp.int32, (m, m), 1)

    def meets(a, b):
        same = (lax.shift_right_logical(a, 4) == (lax.shift_right_logical(b, 1) & 15)) & ((lax.shift_right_logical(a, 1) & 7) == lax.shift_right_logical(b, 5)) & ((a & 1) == (b & 1))
        return jnp.where(same, 1.0, 0.0).astype(BF16)

    spread[...] = meets(a, b)
    unspread[...] = meets(b, a)

    def pack(target, q):
        for j in range(PAIRS):
            lane = slice(j * CHUNK, (j + 1) * CHUNK)
            block = jnp.dot(spread[...], stage[:, lane], preferred_element_type=F32).astype(BF16)
            target[pl.ds(q * SLOTS, SLOTS), :, lane] = block.reshape(SLOTS, 2 * PIECES, CHUNK)

    def unpack(source, q, put):
        for j in range(PAIRS):
            lane = slice(j * CHUNK, (j + 1) * CHUNK)
            block = source[pl.ds(q * SLOTS, SLOTS), :, lane].reshape(m, CHUNK)
            block = jnp.dot(unspread[...], block, preferred_element_type=F32).astype(BF16)
            for c in range(PIECES):
                put(slice(2 * SLOTS * j, 2 * SLOTS * (j + 1)), slice(c * CHUNK, (c + 1) * CHUNK), block[2 * SLOTS * c : 2 * SLOTS * (c + 1)])

    def to_stage(c, value):
        for j in range(PAIRS):
            stage[2 * SLOTS * c : 2 * SLOTS * (c + 1), j * CHUNK : (j + 1) * CHUNK] = value[2 * SLOTS * j : 2 * SLOTS * (j + 1)]

    def remote(source, target, slot, sign, send, recv):
        return pltpu.make_async_remote_copy(
            src_ref=source.at[slot], dst_ref=target.at[slot], send_sem=send, recv_sem=recv,
            device_id=partner(slot, sign), device_id_type=MESH,
        )

    def send_group(source, target, q, sign, send, recv):
        def one(i, carry):
            remote(source, target, q * SLOTS + i, sign, send, recv.at[q]).start()
            return carry

        lax.fori_loop(0, SLOTS - lax.div(q, GROUPS - 1), one, 0)

        @pl.when(q == GROUPS - 1)
        def _():
            pltpu.make_async_copy(source.at[CHIPS - 1], target.at[CHIPS - 1], own_sem).start()

    def wait_group(target, q, recv):
        @pl.when(q < GROUPS - 1)
        def _():
            ref = target.at[pl.ds(0, SLOTS)]
            pltpu.make_async_copy(ref, ref, recv.at[q]).wait()

        @pl.when(q == GROUPS - 1)
        def _():
            ref = target.at[pl.ds(0, SLOTS - 1)]
            pltpu.make_async_copy(ref, ref, recv.at[q]).wait()
            pltpu.make_async_copy(target.at[CHIPS - 1], target.at[CHIPS - 1], own_sem).wait()

    loads()[0].wait()
    pl.semaphore_wait(barrier, CHIPS)

    def dispatch(q, carry):
        for c in range(PIECES):
            value = jnp.dot(pick[q], tok[:, c * CHUNK : (c + 1) * CHUNK], preferred_element_type=F32)
            to_stage(c, value.astype(BF16))
        pack(sent, q)
        send_group(sent, got, q, 1, there_send, there_recv)
        return carry

    lax.fori_loop(0, GROUPS, dispatch, 0)
    for copy in loads()[1:]:
        copy.wait()

    def to_twin(source, target, send, recv):
        return pltpu.make_async_remote_copy(
            src_ref=source, dst_ref=target, send_sem=send, recv_sem=recv, device_id=twin, device_id_type=MESH
        )

    def work(q, carry):
        wait_group(got, q, there_recv)

        def put(r, c, value):
            rows[q, r, c] = value

        unpack(got, q, put)
        over = to_twin(rows.at[q, pl.ds(0, OWN)], rows.at[q, pl.ds(OWN, OWN)], row_send.at[q], row_recv.at[q])
        over.start()
        over.wait()

        def up(t, carry):
            lane = pl.ds(pl.multiple_of(t * 256, 256), 256)
            gate = jnp.dot(rows[q], w_gate[:, lane], preferred_element_type=F32)
            upper = jnp.dot(rows[q], w_up[:, lane], preferred_element_type=F32)
            hidden[:, lane] = (gate / (1.0 + jnp.exp(-gate)) * upper).astype(BF16)
            return carry

        lax.fori_loop(0, 3, up, 0)

        def down(t, carry):
            lane = pl.ds(pl.multiple_of(t * CHUNK, CHUNK), CHUNK)
            part = jnp.dot(hidden[...], w_down[:, lane], preferred_element_type=F32).astype(BF16)
            part_own[:, lane] = part[:OWN]
            part_out[q, :, lane] = part[OWN:]
            return carry

        lax.fori_loop(0, PIECES, down, 0)
        over = to_twin(part_out.at[q], part_in.at[q], part_send.at[q], part_recv.at[q])
        over.start()
        over.wait()
        for c in range(PIECES):
            lane = slice(c * CHUNK, (c + 1) * CHUNK)
            to_stage(c, (part_own[:, lane].astype(F32) + part_in[q, :, lane].astype(F32)).astype(BF16))
        pack(answer, q)
        send_group(answer, back, q, -1, back_send, back_recv)
        return carry

    lax.fori_loop(0, GROUPS, work, 0)

    total[...] = jnp.zeros_like(total)

    def finish(q, carry):
        wait_group(back, q, back_recv)

        def put(r, c, value):
            flat[r, c] = value

        unpack(back, q, put)
        for c in range(PIECES):
            lane = slice(c * CHUNK, (c + 1) * CHUNK)
            for h in range(2):
                total[:, lane] += lax.dot_general(mixing[h, q], flat[:, lane], (((0,), (0,)), ((), ())), preferred_element_type=F32)
        return carry

    lax.fori_loop(0, GROUPS, finish, 0)
    out[...] = total[...].astype(BF16)
    for source, send in ((sent, there_send), (answer, back_send)):
        ref = source.at[pl.ds(0, CHIPS - 1)]
        pltpu.make_async_copy(ref, ref, send).wait()


def body(tokens, expert_ids, gate_scores, w_gate, w_up, w_down):
    rows, width = tokens.shape
    half = w_gate.shape[2]
    blocks = (CHIPS, 2 * PIECES, LANES)
    m = 2 * SLOTS * PIECES
    vmem, hbm = pl.BlockSpec(memory_space=pltpu.VMEM), pl.BlockSpec(memory_space=pl.ANY)
    dma = pltpu.SemaphoreType.DMA
    return pl.pallas_call(
        kernel,
        out_shape=jax.ShapeDtypeStruct((rows, width), BF16),
        in_specs=[vmem, vmem, hbm, hbm, hbm, hbm],
        out_specs=vmem,
        scratch_shapes=[
            pltpu.VMEM((rows, width), BF16),
            pltpu.VMEM((width, half), BF16),
            pltpu.VMEM((width, half), BF16),
            pltpu.VMEM((half, width), BF16),
            pltpu.VMEM(blocks, BF16),
            pltpu.VMEM(blocks, BF16),
            pltpu.VMEM((GROUPS, 2 * OWN, width), BF16),
            pltpu.VMEM((2 * OWN, half), BF16),
            pltpu.VMEM((OWN, width), BF16),
            pltpu.VMEM((GROUPS, OWN, width), BF16),
            pltpu.VMEM((GROUPS, OWN, width), BF16),
            pltpu.VMEM(blocks, BF16),
            pltpu.VMEM(blocks, BF16),
            pltpu.VMEM((GROUPS, OWN, rows), BF16),
            pltpu.VMEM((2, GROUPS, OWN, rows), BF16),
            pltpu.VMEM((m, m), BF16),
            pltpu.VMEM((m, m), BF16),
            pltpu.VMEM((m, LANES), BF16),
            pltpu.VMEM((OWN, width), BF16),
            pltpu.VMEM((rows, width), F32),
            dma((4,)),
            dma, dma((GROUPS,)),
            dma((GROUPS,)), dma((GROUPS,)),
            dma((GROUPS,)), dma((GROUPS,)),
            dma, dma((GROUPS,)),
            dma,
        ],
        compiler_params=pltpu.CompilerParams(collective_id=0, has_side_effects=True, vmem_limit_bytes=60 << 20),
    )(expert_ids.T, gate_scores.T, tokens, w_gate, w_up, w_down)


def solution(mesh):
    split = ("group", "local")
    flat, deep = P(split, None), P(split, None, None)
    return jax.shard_map(
        body, mesh=mesh, in_specs=(flat, flat, flat, deep, deep, deep), out_specs=flat, check_vma=False
    )
```

time: 324 us -> 97.1 us (0.30)
  the two profiles are of different devices: /device:TPU:1 before, /device:TPU:26 now
where the time goes in v1:
time: 97.1 us; the launch traced here: 97 us
  Pallas kernels  94.7 us (98%)
  local copies, waits for them, and re-layouts  2.29 us (2%)
    pallas_call x1, Pallas kernels, body(): pl.pallas_call(kernel, out_shape=jax.ShapeDtypeStruct((rows, width), BF16...  94.7 us
    unnamed x1, local copies, waits for them, and re-layouts  2.29 us

profile of v1, /device:TPU:26, one launch (start us, length us, event | category | flops | bytes accessed | tf_op | source)
XLA Modules:
  0.0 97.0 jit_solution(2787693568549885483)
XLA Ops:
  0.0 94.7 %shard_map.64 = bf16[128,4096]{1,0:T(8,128)(2,1)} custom-call(s32[2,128]{1,0:T(2,128)} %bitcast.2, f32[2,128]{1,0:T(2,128)} %bitcast.3, bf16[128,4096]{1,0:T(8,128)(2,1)} %tok_hbm.1, bf16[1,4096,768]{2,1,0:T(8,128)(2,1)} %gate_hbm.1, bf16[1,4096,768]{2,1,0:T(8,128)(2,1)} %up_hbm.1, bf16[1,768,4096]{2,1,0:T(8,128)(2,1)} %down_hbm.1), custom_call_target="tpu_custom_call" | custom-call | tf_op jit(solution)/shard_map/pallas_call | solution.py:232
  94.7 2.3 %copy.8 = bf16[128,4096]{1,0:T(8,128)(2,1)} copy(bf16[128,4096]{1,0:T(8,128)(2,1)} %shard_map.64) | data formatting | bytes 2097152
